TPU v7x, 32 devices: a whole 2x2x4 slice. The times are simulated.
32 devices in a mesh: section: 4 (over z), ctx: 8 (over y, x, core).
Axes of the slice: x: 2, y: 2, z: 4, core: 2. Of those that a mesh axis runs over, the one named last changes fastest.
Arguments:
- queries: bfloat16 [4, 2048, 3072], P('section', 'ctx'), may hold values from -160 to 160
- keys: bfloat16 [4, 2048, 512], P('section', 'ctx'), may hold values from -48 to 48
- values: bfloat16 [4, 2048, 512], P('section', 'ctx'), may hold values from -15 to 15
- cotangent: bfloat16 [4, 2048, 3072], P('section', 'ctx'), may hold values from -6 to 6
- router_logits: bfloat16 [4, 2048], P('section', 'ctx'), may hold values from -8 to 8
- positions: int32 [4, 2048], P('section', 'ctx'), may hold values from -1 to 8191, as said below
- counts: int32 [4, 8], P('section', 'ctx'), may hold values from 0 to 2, as said below
Outputs:
- handed: bfloat16 [4, 2048, 3072], P('section', 'ctx')
- value_grad: bfloat16 [4, 2048, 512], P('section', 'ctx')
- gate_grad: bfloat16 [4, 2048], P('section', 'ctx')
Inputs may be any that keep to these rules, and one draw needn't show every extreme that they name: For every micro-batch and every shard c, the counts of shards 0 to c sum to c + 1 or c + 2; shard 0 holds 2 blocks; all counts of a micro-batch sum to 8. In shard c's slots, the first counts * 128 hold distinct positions in increasing order, all within c * 1024 to (c + 1) * 1024 - 1; the other slots hold -1.
All inputs are finite; a program needn't handle non-finite values.
Results may differ from a plain program's by a relative error of at most 0.0066.
Values may be sent and summed in bfloat16 or wider, within the bound.
No kernel may reach another device: no remote copies, remote signals or barrier semaphores. Data moves between devices by JAX's collectives and lax.ppermute only.
A program may use at most 128 MiB of HBM per device.

v0:
```python
import math

import jax
import jax.numpy as jnp
from jax import lax
from jax.experimental import pallas as pl
from jax.experimental.pallas import tpu as pltpu
from jax.sharding import PartitionSpec as P

QUERY_HEADS = 24
KEY_VALUE_HEADS = 4
HEAD_SIZE = 128
BLOCK_ROWS = 128
MAXB = 2

CORES = 2
GROUP = QUERY_HEADS // KEY_VALUE_HEADS
LOCAL_HEADS = KEY_VALUE_HEADS // CORES
GROUP_WIDTH = GROUP * HEAD_SIZE
HALF_QUERY = LOCAL_HEADS * GROUP_WIDTH
HALF_KEY = LOCAL_HEADS * HEAD_SIZE
CHIP_BLOCKS = 2 * MAXB - 1
CHIP_ROWS = CHIP_BLOCKS * BLOCK_ROWS
META_ROWS = 16
SLOTS = MAXB * BLOCK_ROWS
MASKED = -1e30
VMEM_LIMIT = 48 * 1024 * 1024
f32 = jnp.float32
bf16 = jnp.bfloat16
i32 = jnp.int32
PAYLOAD = 2 * HALF_KEY + HEAD_SIZE


def params(limit):
    return pltpu.CompilerParams(vmem_limit_bytes=limit)


def whole(shape):
    return pl.BlockSpec(shape, lambda i, s: (0,) * len(shape))


def call(body, scalars, grid_in, operands, outs, out_specs, scratch=(), flops=0, moved=0, limit=VMEM_LIMIT, aliases={}):
    return pl.pallas_call(
        body,
        grid_spec=pltpu.PrefetchScalarGridSpec(
            num_scalar_prefetch=1,
            grid=(1,),
            in_specs=grid_in,
            out_specs=out_specs,
            scratch_shapes=list(scratch),
        ),
        out_shape=outs,
        compiler_params=params(limit),
        input_output_aliases=aliases,
        cost_estimate=pl.CostEstimate(flops=flops, bytes_accessed=moved, transcendentals=0),
    )(scalars, *operands)


def shape(rows, columns, kind=bf16):
    return jax.ShapeDtypeStruct((rows, columns), kind)


def rows_of(block):
    return pl.ds(pl.multiple_of(block * BLOCK_ROWS, BLOCK_ROWS), BLOCK_ROWS)


def my_core():
    return lax.axis_index("ctx") % CORES


def half(source, width, core):
    return source.at[0, :, pl.ds(pl.multiple_of(core * width, width), width)]


def pack_kernel(s, k, v, logits, out, column, own_kv, flat, arrived):
    core = my_core()
    moves = (
        (logits, flat),
        (half(k, HALF_KEY, 1 - core), out.at[:, 0:HALF_KEY]),
        (half(v, HALF_KEY, 1 - core), out.at[:, HALF_KEY : 2 * HALF_KEY]),
        (half(k, HALF_KEY, core), own_kv.at[:, 0:HALF_KEY]),
        (half(v, HALF_KEY, core), own_kv.at[:, HALF_KEY:]),
    )
    copies = [pltpu.make_async_copy(source, target, arrived.at[n]) for n, (source, target) in enumerate(moves)]
    for copy in copies:
        copy.start()
    copies[0].wait()
    count = s[0]
    for b in range(MAXB):
        row = flat[0:1, b * BLOCK_ROWS : (b + 1) * BLOCK_ROWS].astype(f32)
        tall = jnp.broadcast_to(row, (BLOCK_ROWS, BLOCK_ROWS)).T
        lane = lax.broadcasted_iota(i32, (BLOCK_ROWS, HEAD_SIZE), 1)
        rows = slice(b * BLOCK_ROWS, (b + 1) * BLOCK_ROWS)
        meta = jnp.where(lane < HEAD_SIZE // 2, tall, count.astype(f32)).astype(bf16)
        out[rows, 2 * HALF_KEY :] = meta
        column[rows, :] = meta
    for copy in copies[1:]:
        copy.wait()


def halves_kernel(s, q, cot, after, mine, theirs, arrived):
    core = my_core()
    copies = [
        pltpu.make_async_copy(
            half(source, HALF_QUERY, at), target.at[:, n * HALF_QUERY : (n + 1) * HALF_QUERY], arrived.at[n, m]
        )
        for n, source in enumerate((q, cot))
        for m, (at, target) in enumerate(((1 - core, theirs), (core, mine)))
    ]
    for copy in copies:
        copy.start()
    for copy in copies:
        copy.wait()


def pass_kernel(s, *refs):
    pass


def passed(scalars, arrays):
    anywhere = [pl.BlockSpec(memory_space=pl.ANY)] * len(arrays)
    return call(
        pass_kernel,
        scalars,
        anywhere,
        tuple(arrays),
        tuple(jax.ShapeDtypeStruct(x.shape, x.dtype) for x in arrays),
        tuple(anywhere),
        flops=15 * 10**9,
        aliases={n + 1: n for n in range(len(arrays))},
    )


def as_scalar(x):
    return jnp.max(x.astype(f32)).astype(i32)


def chip_counts(s, meta):
    own = s[0]
    other = as_scalar(meta[0:META_ROWS, HEAD_SIZE // 2 :])
    first = jnp.where(my_core() == 0, own, other)
    return first, own + other


def place_of(block, first, core):
    on_first = block < first
    slot = jnp.where(on_first, block, block - first)
    mine = jnp.where(on_first, 0, 1) == core
    return mine, slot


def chip_kernel(s, k, v, kr, vr, meta, *outs):
    *outs, pair = outs
    first, live = chip_counts(s, meta)
    lane = lax.broadcasted_iota(i32, (META_ROWS, HEAD_SIZE), 1)
    pair[...] = jnp.where(lane < HEAD_SIZE // 2, first.astype(f32), (live - first).astype(f32)).astype(bf16)
    for b in range(CHIP_BLOCKS):
        mine, slot = place_of(b, first, my_core())
        rows = slice(b * BLOCK_ROWS, (b + 1) * BLOCK_ROWS)

        def copy(keys, vals):
            for h in range(LOCAL_HEADS):
                cols = slice(h * HEAD_SIZE, (h + 1) * HEAD_SIZE)
                outs[h][rows, 0:HEAD_SIZE] = keys[rows_of(slot), cols]
                outs[h][rows, HEAD_SIZE:] = vals[rows_of(slot), cols]

        @pl.when(jnp.logical_and(b < live, mine))
        def _():
            copy(k, v)

        @pl.when(jnp.logical_and(b < live, jnp.logical_not(mine)))
        def _():
            copy(kr, vr)

        @pl.when(b >= live)
        def _():
            for h in range(LOCAL_HEADS):
                outs[h][rows, :] = jnp.zeros((BLOCK_ROWS, 2 * HEAD_SIZE), bf16)

    for h in range(LOCAL_HEADS):
        outs[h][CHIP_ROWS:, :] = jnp.broadcast_to(live.astype(f32), (META_ROWS, 2 * HEAD_SIZE)).astype(bf16)


def attend_kernel(chips, chunk, has_prior, s, *refs):
    q, qr, cot, cotr, column, columnr = refs[:6]
    at = 6
    kv = refs[at : at + chips]
    at += chips
    prior = refs[at : at + chips] if has_prior else None
    at += chips if has_prior else 0
    branch, gate_part = refs[at : at + 2]
    at += 2
    dvs = refs[at : at + chips]
    at += chips
    kd, vd, qs, og, probs, acc, dv = refs[at:]
    steps = kd.shape[0] // chunk

    first, live = chip_counts(s, columnr)
    core = my_core()
    ones = jnp.ones((BLOCK_ROWS, HEAD_SIZE), bf16)
    vd[...] = jnp.zeros_like(vd)
    dv[...] = jnp.zeros_like(dv)

    held = [live] + [as_scalar(kv[d][CHIP_ROWS:, 0:HEAD_SIZE]) for d in range(1, chips)]
    starts = [None] * chips
    position = jnp.int32(0)
    for d in list(range(1, chips)) + [0]:
        starts[d] = position
        for b in range(CHIP_BLOCKS):

            @pl.when(b < held[d])
            def _(d=d, b=b, position=position):
                rows = slice(b * BLOCK_ROWS, (b + 1) * BLOCK_ROWS)
                to = rows_of(position + b)
                kd[to, :] = kv[d][rows, 0:HEAD_SIZE]
                vd[to, 0:HEAD_SIZE] = kv[d][rows, HEAD_SIZE:]
                vd[to, HEAD_SIZE:] = ones

        position = position + held[d]
    base = starts[0]
    scale = math.log2(math.e) / math.sqrt(HEAD_SIZE)
    tall = GROUP * BLOCK_ROWS

    def one_block(b, _):
        mine, slot = place_of(b, first, core)
        here = rows_of(slot)

        @pl.when(mine)
        def _():
            for i in range(GROUP):
                qs[i * BLOCK_ROWS : (i + 1) * BLOCK_ROWS, :] = q[here, i * HEAD_SIZE : (i + 1) * HEAD_SIZE]

        @pl.when(jnp.logical_not(mine))
        def _():
            for i in range(GROUP):
                qs[i * BLOCK_ROWS : (i + 1) * BLOCK_ROWS, :] = qr[here, i * HEAD_SIZE : (i + 1) * HEAD_SIZE]

        t = base + b

        def finish(grad, col):
            logit = jnp.broadcast_to(col[here, 0:1].astype(f32), (BLOCK_ROWS, HEAD_SIZE))
            gate = 1.0 / (1.0 + jnp.exp(-logit))
            total = jnp.zeros((BLOCK_ROWS, HEAD_SIZE), f32)
            for i in range(GROUP):
                rows = slice(i * BLOCK_ROWS, (i + 1) * BLOCK_ROWS)
                cols = slice(i * HEAD_SIZE, (i + 1) * HEAD_SIZE)
                inverse = 1.0 / acc[rows, HEAD_SIZE:]
                attended = acc[rows, 0:HEAD_SIZE] * inverse
                branch[rows_of(b), cols] = (gate * attended).astype(bf16)
                g = grad[here, cols].astype(f32)
                total = total + g * attended
                og[rows, :] = (gate * g * inverse).astype(bf16)
            gate_part[rows_of(b), :] = total

        def sweep(reach):
            key = lax.broadcasted_iota(i32, (BLOCK_ROWS, chunk), 1) + (reach - chunk)
            row = t * BLOCK_ROWS + lax.broadcasted_iota(i32, (BLOCK_ROWS, chunk), 0)
            allowed = key <= row
            for c in range(GROUP):
                w = slice(c * BLOCK_ROWS, (c + 1) * BLOCK_ROWS)
                x = lax.dot_general(
                    qs[w, :], kd[0:reach, :], (((1,), (1,)), ((), ())), preferred_element_type=f32
                )
                tail = jnp.where(allowed, x[:, reach - chunk :], MASKED)
                x = tail if reach == chunk else jnp.concatenate([x[:, : reach - chunk], tail], axis=1)
                p = jnp.exp2((x - jnp.max(x, axis=1, keepdims=True)) * scale).astype(bf16)
                probs[w, 0:reach] = p
                acc[w, :] = jnp.dot(p, vd[0:reach, :], preferred_element_type=f32)

            @pl.when(mine)
            def _():
                finish(cot, column)

            @pl.when(jnp.logical_not(mine))
            def _():
                finish(cotr, columnr)

            width = min(2 * BLOCK_ROWS, chunk)
            for c in range(reach // width):
                w = slice(c * width, (c + 1) * width)
                dv[w, :] += lax.dot_general(
                    probs[:, w], og[...], (((0,), (0,)), ((), ())), preferred_element_type=f32
                )

        last = t * BLOCK_ROWS // chunk
        for j in range(steps):

            @pl.when(last == j)
            def _(j=j):
                sweep((j + 1) * chunk)

        return 0

    lax.fori_loop(0, live, one_block, 0)
    if branch.shape[0] > CHIP_ROWS:
        lane = lax.broadcasted_iota(i32, (META_ROWS, GROUP_WIDTH), 1)
        counted = jnp.where(lane < HEAD_SIZE // 2, first.astype(f32), (live - first).astype(f32))
        branch[CHIP_ROWS:, :] = counted.astype(bf16)

    for b in range(CHIP_BLOCKS):
        rows = slice(b * BLOCK_ROWS, (b + 1) * BLOCK_ROWS)

        @pl.when(b >= live)
        def _():
            branch[rows, :] = jnp.zeros((BLOCK_ROWS, GROUP_WIDTH), bf16)
            gate_part[rows, :] = jnp.zeros((BLOCK_ROWS, HEAD_SIZE), f32)

        for d in range(chips):
            cols = slice(0, HEAD_SIZE)
            if has_prior:
                dvs[d][rows, 0:HEAD_SIZE] = prior[d][rows, :]
                cols = slice(HEAD_SIZE, 2 * HEAD_SIZE)

            @pl.when(b < held[d])
            def _():
                dvs[d][rows, cols] = dv[rows_of(starts[d] + b), :].astype(dvs[d].dtype)

            @pl.when(b >= held[d])
            def _():
                dvs[d][rows, cols] = jnp.zeros((BLOCK_ROWS, HEAD_SIZE), dvs[d].dtype)


def spread(slot, core, first, second, write, clear):
    held = jnp.where(core == 0, first, second)
    block = jnp.where(core == 0, slot, first + slot)

    @pl.when(slot < held)
    def _():
        write(rows_of(jnp.minimum(block, CHIP_BLOCKS - 1)))

    @pl.when(slot >= held)
    def _():
        clear()


def branch_kernel(s, part, pair, mine, theirs):
    first = as_scalar(pair[:, 0 : HEAD_SIZE // 2])
    second = as_scalar(pair[:, HEAD_SIZE // 2 :])
    for out, core in ((mine, my_core()), (theirs, 1 - my_core())):
        for slot in range(MAXB):
            rows = slice(slot * BLOCK_ROWS, (slot + 1) * BLOCK_ROWS)

            def write(source):
                out[rows, :] = part[source, :]

            def clear():
                out[rows, :] = jnp.zeros((BLOCK_ROWS, GROUP_WIDTH), bf16)

            spread(slot, core, first, second, write, clear)


def join_kernel(h, s, mine, theirs, *refs):
    out, sent = refs[-2:]
    core = my_core()
    copies = []
    for n, (at, part) in enumerate(((core, mine), (1 - core, theirs))):
        start = pl.multiple_of(at * HALF_QUERY + h * GROUP_WIDTH, HEAD_SIZE)
        copies.append(pltpu.make_async_copy(part, out.at[:, pl.ds(start, GROUP_WIDTH)], sent.at[n]))
        copies[-1].start()
    for copy in copies:
        copy.wait()


def gradient_kernel(chips, s, *refs):
    columnr = refs[0]
    own = refs[1]
    arrived = refs[2 : 1 + chips]
    gate_parts = refs[1 + chips : 1 + chips + LOCAL_HEADS]
    mine, gate_mine, theirs = refs[1 + chips + LOCAL_HEADS :]
    first, live = chip_counts(s, columnr)
    second = live - first
    for which, core in ((0, my_core()), (1, 1 - my_core())):
        for slot in range(MAXB):
            rows = slice(slot * BLOCK_ROWS, (slot + 1) * BLOCK_ROWS)

            def write(source):
                total = own[source, :]
                for other in arrived:
                    total = total + other[source, :].astype(f32)
                summed = gate_parts[0][source, :]
                for h in range(1, LOCAL_HEADS):
                    summed = summed + gate_parts[h][source, :]
                summed = jnp.broadcast_to(jnp.sum(summed, axis=1, keepdims=True), (BLOCK_ROWS, HEAD_SIZE))
                if which == 0:
                    mine[rows, :] = total.astype(bf16)
                    gate_mine[rows, :] = summed
                else:
                    theirs[rows, 0:HALF_KEY] = total.astype(bf16)
                    high = summed.astype(bf16)
                    low = (summed - high.astype(f32)).astype(bf16)
                    lane = lax.broadcasted_iota(i32, (BLOCK_ROWS, HEAD_SIZE), 1)
                    theirs[rows, HALF_KEY:] = jnp.where(lane < HEAD_SIZE // 2, high, low)

            def clear():
                if which == 0:
                    mine[rows, :] = jnp.zeros((BLOCK_ROWS, HALF_KEY), bf16)
                    gate_mine[rows, :] = jnp.zeros((BLOCK_ROWS, HEAD_SIZE), f32)
                else:
                    theirs[rows, :] = jnp.zeros((BLOCK_ROWS, HALF_KEY + HEAD_SIZE), bf16)

            spread(slot, core, first, second, write, clear)


def finish_kernel(s, mine, gate_mine, theirs, column, out, gate_out):
    @pl.when(my_core() == 0)
    def _():
        out[:, 0:HALF_KEY] = mine[...]
        out[:, HALF_KEY:] = theirs[:, 0:HALF_KEY]

    @pl.when(my_core() != 0)
    def _():
        out[:, 0:HALF_KEY] = theirs[:, 0:HALF_KEY]
        out[:, HALF_KEY:] = mine[...]

    half = HALF_KEY + HEAD_SIZE // 2
    for b in range(MAXB):
        rows = slice(b * BLOCK_ROWS, (b + 1) * BLOCK_ROWS)
        total = (
            gate_mine[rows, 0:1]
            + theirs[rows, HALF_KEY : HALF_KEY + 1].astype(f32)
            + theirs[rows, half : half + 1].astype(f32)
        )
        logit = column[rows, 0:1].astype(f32)
        gate = 1.0 / (1.0 + jnp.exp(-logit))
        full = jnp.broadcast_to(gate * (1.0 - gate) * total, (BLOCK_ROWS, HEAD_SIZE)).T
        gate_out[0:1, rows] = full[0:1, :].astype(bf16)


def fixed(width, at):
    return pl.BlockSpec((SLOTS, width), lambda i, s: (0, at))


def attend(chips, shards, h, scalars, *operands):
    steps = min(4, shards)
    chunk = -(-shards // steps) * BLOCK_ROWS
    reach = steps * chunk
    tall = GROUP * BLOCK_ROWS
    packed_rows = CHIP_ROWS + META_ROWS
    prior = len(operands) - 6 - chips
    sent_rows = CHIP_ROWS if h else packed_rows
    width = HEAD_SIZE * (2 if prior else 1)
    own_at = fixed(GROUP_WIDTH, h)
    column_spec = fixed(HEAD_SIZE, 2 * HALF_KEY // HEAD_SIZE)
    cot_at = fixed(GROUP_WIDTH, LOCAL_HEADS + h)
    return call(
        lambda *refs: attend_kernel(chips, chunk, bool(prior), *refs),
        scalars,
        [own_at, own_at, cot_at, cot_at, whole((SLOTS, HEAD_SIZE)), column_spec]
        + [whole((packed_rows, 2 * HEAD_SIZE))] * chips
        + [whole((CHIP_ROWS, HEAD_SIZE))] * prior,
        operands,
        (shape(sent_rows, GROUP_WIDTH), shape(CHIP_ROWS, HEAD_SIZE, f32), shape(CHIP_ROWS, width, f32))
        + tuple(shape(CHIP_ROWS, width) for _ in range(chips - 1)),
        (whole((sent_rows, GROUP_WIDTH)), whole((CHIP_ROWS, HEAD_SIZE))) + (whole((CHIP_ROWS, width)),) * chips,
        scratch=(
            pltpu.VMEM((reach, HEAD_SIZE), bf16),
            pltpu.VMEM((reach, 2 * HEAD_SIZE), bf16),
            pltpu.VMEM((tall, HEAD_SIZE), bf16),
            pltpu.VMEM((tall, HEAD_SIZE), bf16),
            pltpu.VMEM((tall, reach), bf16),
            pltpu.VMEM((tall, 2 * HEAD_SIZE), f32),
            pltpu.VMEM((reach, HEAD_SIZE), f32),
        ),
        flops=100 * tall * HEAD_SIZE * reach,
        moved=6 * packed_rows * GROUP_WIDTH,
    )


def local(queries, keys, values, cotangent, router_logits, positions, counts):
    shards = lax.axis_size("ctx")
    sections = lax.axis_size("section")
    chips = shards // CORES
    scalars = counts[0]
    def swap(x):
        return lax.ppermute(x, "ctx", [(i, i ^ 1) for i in range(shards)])

    def onward(x, by):
        step = by * CORES
        return lax.ppermute(x, "ctx", [(i, i + step) for i in range(shards) if 0 <= i + step < shards])

    def section_on(x):
        return lax.ppermute(x, "section", [(i, (i + 1) % sections) for i in range(sections)])

    def near(x):
        return pltpu.with_memory_space_constraint(x, pltpu.HBM)

    far = pl.BlockSpec(memory_space=pltpu.HBM)
    column_spec = fixed(HEAD_SIZE, 2 * HALF_KEY // HEAD_SIZE)
    payload, column, own_kv = call(
        pack_kernel,
        scalars,
        [far, far, far],
        (near(keys), near(values), near(router_logits)),
        (shape(SLOTS, PAYLOAD), shape(SLOTS, HEAD_SIZE), shape(SLOTS, 2 * HALF_KEY)),
        tuple(whole((SLOTS, width)) for width in (PAYLOAD, HEAD_SIZE, 2 * HALF_KEY)),
        scratch=(pltpu.VMEM((1, SLOTS), bf16), pltpu.SemaphoreType.DMA((5,))),
        moved=4 * SLOTS * PAYLOAD * 2,
    )
    other = swap(payload)
    packed_rows = CHIP_ROWS + META_ROWS
    *packed, pair = call(
        chip_kernel,
        scalars,
        [fixed(HALF_KEY, 0), fixed(HALF_KEY, 1), fixed(HALF_KEY, 0), fixed(HALF_KEY, 1), column_spec],
        (own_kv, own_kv, other, other, other),
        tuple(shape(packed_rows, 2 * HEAD_SIZE) for _ in range(LOCAL_HEADS)) + (shape(META_ROWS, HEAD_SIZE),),
        tuple(whole((packed_rows, 2 * HEAD_SIZE)) for _ in range(LOCAL_HEADS)) + (whole((META_ROWS, HEAD_SIZE)),),
        moved=4 * packed_rows * HALF_KEY * 2,
    )
    gathered = [[packed[0]] + [onward(packed[0], d) for d in range(1, chips)]]
    own, theirs = call(
        halves_kernel,
        scalars,
        [far, far, pl.BlockSpec(memory_space=pl.ANY)],
        (near(queries), near(cotangent), swap(pair)),
        (shape(SLOTS, 2 * HALF_QUERY), shape(SLOTS, 2 * HALF_QUERY)),
        (whole((SLOTS, 2 * HALF_QUERY)), whole((SLOTS, 2 * HALF_QUERY))),
        scratch=(pltpu.SemaphoreType.DMA((2, 2)),),
        moved=0,
    )
    for h in range(1, LOCAL_HEADS):
        packed[h], theirs = lax.optimization_barrier((packed[h], theirs))
        gathered.append([packed[h]] + [onward(packed[h], d) for d in range(1, chips)])
    swapped = swap(theirs)
    if chips > 1:
        gathered[0][1:] = passed(scalars, gathered[0][1:])
    prior = []
    branches, gate_parts = [], []
    for h in range(LOCAL_HEADS):
        results = attend(chips, shards, h, scalars, own, swapped, own, swapped, column, other, *gathered[h], *prior)
        branches.append(section_on(results[0]))
        gate_parts.append(results[1])
        prior = results[2:]
    returned = [onward(prior[d], -d) for d in range(1, chips)]
    branches[0], *returned = lax.optimization_barrier((branches[0], *returned))
    grad_mine, gate_mine, grad_theirs = call(
        lambda *refs: gradient_kernel(chips, *refs),
        scalars,
        [column_spec]
        + [whole((CHIP_ROWS, HALF_KEY))] * chips
        + [whole((CHIP_ROWS, HEAD_SIZE))] * LOCAL_HEADS,
        (other, prior[0], *returned, *gate_parts),
        (shape(SLOTS, HALF_KEY), shape(SLOTS, HEAD_SIZE, f32), shape(SLOTS, HALF_KEY + HEAD_SIZE)),
        (whole((SLOTS, HALF_KEY)), whole((SLOTS, HEAD_SIZE)), whole((SLOTS, HALF_KEY + HEAD_SIZE))),
        moved=8 * CHIP_ROWS * HALF_KEY,
    )
    grad_other = swap(grad_theirs)
    value_grad, gate_grad = call(
        finish_kernel,
        scalars,
        [
            whole((SLOTS, HALF_KEY)),
            whole((SLOTS, HEAD_SIZE)),
            whole((SLOTS, HALF_KEY + HEAD_SIZE)),
            whole((SLOTS, HEAD_SIZE)),
        ],
        (grad_mine, gate_mine, grad_other, column),
        (shape(SLOTS, CORES * HALF_KEY), shape(1, SLOTS)),
        (whole((SLOTS, CORES * HALF_KEY)), whole((1, SLOTS))),
        moved=8 * SLOTS * HALF_KEY,
    )
    branches[-1], value_grad = lax.optimization_barrier((branches[-1], value_grad))
    handed = ()
    for h in range(LOCAL_HEADS):
        mine, theirs = call(
            branch_kernel,
            scalars,
            [
                whole((CHIP_ROWS, GROUP_WIDTH)),
                pl.BlockSpec((META_ROWS, HEAD_SIZE), lambda i, s: (CHIP_ROWS // META_ROWS, 0)),
            ],
            (branches[h], branches[0]),
            (shape(SLOTS, GROUP_WIDTH), shape(SLOTS, GROUP_WIDTH)),
            (whole((SLOTS, GROUP_WIDTH)), whole((SLOTS, GROUP_WIDTH))),
            moved=7 * SLOTS * HALF_QUERY,
        )
        handed = (
            call(
                lambda *refs, h=h: join_kernel(h, *refs),
                scalars,
                [whole((SLOTS, GROUP_WIDTH))] * 2 + [far] * len(handed),
                (mine, swap(theirs), *handed),
                shape(SLOTS, CORES * HALF_QUERY),
                far,
                scratch=(pltpu.SemaphoreType.DMA((2,)),),
                moved=8 * SLOTS * GROUP_WIDTH,
                aliases={3: 0} if handed else {},
            ),
        )
    (handed,) = handed
    return (handed[None], value_grad[None], gate_grad)


def solution(mesh):
    rows = P("section", "ctx", None)
    flat = P("section", "ctx")
    return jax.shard_map(
        local,
        mesh=mesh,
        in_specs=(rows, rows, rows, rows, flat, flat, flat),
        out_specs=(rows, rows, flat),
        check_vma=False,
    )
```

profile of v0, /device:TPU:0, one launch (start us, length us, event | category | flops | bytes accessed | tf_op | source)
XLA Modules:
  0.0 60.0 jit_solution(914084511058435717)
XLA Ops:
  1.3 1.2 %shard_map.85 = (bf16[256,640]{1,0:T(8,128)(2,1)S(1)}, bf16[256,128]{1,0:T(8,128)(2,1)S(1)}, bf16[256,512]{1,0:T(8,128)(2,1)S(1)}) custom-call(s32[1]{0:T(128)} %bitcast.3.s, bf16[1,256,512]{2,1,0:T(8,128)(2,1)} %k.1, bf16[1,256,512]{2,1,0:T(8,128)(2,1)} %v.1, bf16[1,256]{1,0:T(2,128)(2,1)} %logits.1), custom_call_target="tpu_custom_call" | custom-call | bytes 1310720 | tf_op jit(solution)/shard_map/pallas_call | solution.py:43
  2.4 0.5 collective-permute-start
  3.0 1.3 %collective-permute-done.kr.vr.meta.refs_6_.refs_1_ = bf16[256,640]{1,0:T(8,128)(2,1)S(1)} collective-permute-done((bf16[256,640]{1,0:T(8,128)(2,1)S(1)}, bf16[256,640]{1,0:T(8,128)(2,1)S(1)}, u32[]{:S(2)}, u32[]{:S(2)}) %collective-permute-start) | collective-permute-done | bytes 327712 | tf_op jit(solution)/shard_map/ppermute | solution.py:475
  4.2 0.3 shard_map.86
  4.5 5.7 %collective-permute-start.8 = (bf16[400,256]{1,0:T(8,128)(2,1)S(1)}, bf16[400,256]{1,0:T(8,128)(2,1)S(1)}, u32[]{:S(2)}, u32[]{:S(2)}) collective-permute-start(bf16[400,256]{1,0:T(8,128)(2,1)S(1)} %get-tuple-element.52.refs_7_), channel_id=1, source_target_pairs={{0,6},{1,7},{8,14},{9,15},{16,22},{17,23},{24,30},{25,31}} | collective-permute-start | bytes 614408 | tf_op jit(solution)/shard_map/ppermute | solution.py:479
  10.2 1.3 %collective-permute-start.7 = (bf16[400,256]{1,0:T(8,128)(2,1)S(1)}, bf16[400,256]{1,0:T(8,128)(2,1)S(1)}, u32[]{:S(2)}, u32[]{:S(2)}) collective-permute-start(bf16[400,256]{1,0:T(8,128)(2,1)S(1)} %get-tuple-element.52.refs_7_), channel_id=1, source_target_pairs={{0,4},{1,5},{2,6},{3,7},{8,12},{9,13},{10,14},{11,15},{16,20},{17,... | collective-permute-start | bytes 614408 | tf_op jit(solution)/shard_map/ppermute | solution.py:479
  11.5 2.5 %collective-permute-start.6 = (bf16[400,256]{1,0:T(8,128)(2,1)S(1)}, bf16[400,256]{1,0:T(8,128)(2,1)S(1)}, u32[]{:S(2)}, u32[]{:S(2)}) collective-permute-start(bf16[400,256]{1,0:T(8,128)(2,1)S(1)} %get-tuple-element.52.refs_7_), channel_id=1, source_target_pairs={{0,2},{1,3},{2,4},{3,5},{4,6},{5,7},{8,10},{9,11},{10,12},{11,13},... | collective-permute-start | bytes 614408 | tf_op jit(solution)/shard_map/ppermute | solution.py:479
  14.0 0.1 collective-permute-start.1
  14.1 1.2 %collective-permute-done.1.after = bf16[16,128]{1,0:T(8,128)(2,1)S(1)} collective-permute-done((bf16[16,128]{1,0:T(8,128)(2,1)S(1)}, bf16[16,128]{1,0:T(8,128)(2,1)S(1)}, u32[]{:S(2)}, u32[]{:S(2)}) %collective-permute-start.1) | collective-permute-done | bytes 4128 | tf_op jit(solution)/shard_map/ppermute | solution.py:475
  15.2 1.9 %shard_map.87 = (bf16[256,3072]{1,0:T(8,128)(2,1)S(1)}, bf16[256,3072]{1,0:T(8,128)(2,1)S(1)}) custom-call(s32[1]{0:T(128)} %bitcast.5.s, bf16[1,256,3072]{2,1,0:T(8,128)(2,1)} %q.1, bf16[1,256,3072]{2,1,0:T(8,128)(2,1)} %cot.1, bf16[16,128]{1,0:T(8,128)(2,1)S(1)} %collective-permute-done.1.after), custom_call_target="tpu_custom_call" | custom-call | tf_op jit(solution)/shard_map/pallas_call | solution.py:43
  17.1 0.2 collective-permute-start.2
  17.3 1.3 %collective-permute-start.5 = (bf16[400,256]{1,0:T(8,128)(2,1)S(1)}, bf16[400,256]{1,0:T(8,128)(2,1)S(1)}, u32[]{:S(2)}, u32[]{:S(2)}) collective-permute-start(bf16[400,256]{1,0:T(8,128)(2,1)S(1)} %get-tuple-element.51.refs_7_), channel_id=1, source_target_pairs={{0,6},{1,7},{8,14},{9,15},{16,22},{17,23},{24,30},{25,31}} | collective-permute-start | bytes 614408 | tf_op jit(solution)/shard_map/ppermute | solution.py:479
  18.6 0.0 collective-permute-done.8.refs_2_
  18.7 1.3 %collective-permute-start.4 = (bf16[400,256]{1,0:T(8,128)(2,1)S(1)}, bf16[400,256]{1,0:T(8,128)(2,1)S(1)}, u32[]{:S(2)}, u32[]{:S(2)}) collective-permute-start(bf16[400,256]{1,0:T(8,128)(2,1)S(1)} %get-tuple-element.51.refs_7_), channel_id=1, source_target_pairs={{0,4},{1,5},{2,6},{3,7},{8,12},{9,13},{10,14},{11,15},{16,20},{17,... | collective-permute-start | bytes 614408 | tf_op jit(solution)/shard_map/ppermute | solution.py:479
  20.0 0.6 collective-permute-done.7.refs_1_
  20.5 2.9 %collective-permute-start.3 = (bf16[400,256]{1,0:T(8,128)(2,1)S(1)}, bf16[400,256]{1,0:T(8,128)(2,1)S(1)}, u32[]{:S(2)}, u32[]{:S(2)}) collective-permute-start(bf16[400,256]{1,0:T(8,128)(2,1)S(1)} %get-tuple-element.51.refs_7_), channel_id=1, source_target_pairs={{0,2},{1,3},{2,4},{3,5},{4,6},{5,7},{8,10},{9,11},{10,12},{11,13},... | collective-permute-start | bytes 614408 | tf_op jit(solution)/shard_map/ppermute | solution.py:479
  23.5 0.0 collective-permute-done.6.refs_0_
  23.5 0.0 collective-permute-done.2.refs_2_.refs_4_
  23.5 0.0 copy-start
  23.5 4.2 %shard_map.89 = (bf16[400,768]{1,0:T(8,128)(2,1)S(1)}, f32[384,128]{1,0:T(8,128)S(1)}, f32[384,128]{1,0:T(8,128)S(1)}, bf16[384,128]{1,0:T(8,128)(2,1)S(1)}, bf1...) custom-call(s32[1]{0:T(128)} %bitcast.7.refs_0_, bf16[256,3072]{1,0:T(8,128)(2,1)S(1)} %get-tuple-element.46.refs_1_.refs_3_, ...), custom_call_target="tpu_custom_call" | custom-call | flops 10066329600 | bytes 1843200 | tf_op jit(solution)/shard_map/pallas_call | solution.py:43
  27.7 0.0 copy-done
  27.8 0.1 collective-permute-start.10
  27.9 0.0 collective-permute-done.5.refs_10_
  27.9 0.0 collective-permute-done.4.refs_9_
  27.9 0.3 collective-permute-done.3.refs_8_
  28.2 5.5 %shard_map.90 = (bf16[384,768]{1,0:T(8,128)(2,1)S(1)}, f32[384,128]{1,0:T(8,128)S(1)}, f32[384,256]{1,0:T(8,128)S(1)}, bf16[384,256]{1,0:T(8,128)(2,1)S(1)}, bf1...) custom-call(s32[1]{0:T(128)} %bitcast.8.refs_0_, bf16[256,3072]{1,0:T(8,128)(2,1)S(1)} %get-tuple-element.46.refs_1_.refs_3_, ...), custom_call_target="tpu_custom_call" | custom-call | flops 10066329600 | bytes 1843200 | tf_op jit(solution)/shard_map/pallas_call | solution.py:43
  33.7 0.1 collective-permute-start.9
  33.9 1.3 %collective-permute-start.11 = (bf16[384,256]{1,0:T(8,128)(2,1)S(1)}, bf16[384,256]{1,0:T(8,128)(2,1)S(1)}, u32[]{:S(2)}, u32[]{:S(2)}) collective-permute-start(bf16[384,256]{1,0:T(8,128)(2,1)S(1)} %get-tuple-element.63), channel_id=1, source_target_pairs={{2,0},{3,1},{4,2},{5,3},{6,4},{7,5},{10,8},{11,9},{12,10},{13,11},... | collective-permute-start | bytes 589832 | tf_op jit(solution)/shard_map/ppermute | solution.py:479
  35.1 1.3 %collective-permute-start.12 = (bf16[384,256]{1,0:T(8,128)(2,1)S(1)}, bf16[384,256]{1,0:T(8,128)(2,1)S(1)}, u32[]{:S(2)}, u32[]{:S(2)}) collective-permute-start(bf16[384,256]{1,0:T(8,128)(2,1)S(1)} %get-tuple-element.64), channel_id=1, source_target_pairs={{4,0},{5,1},{6,2},{7,3},{12,8},{13,9},{14,10},{15,11},{20,16},{21,... | collective-permute-start | bytes 589832 | tf_op jit(solution)/shard_map/ppermute | solution.py:479
  36.4 1.3 %collective-permute-start.13 = (bf16[384,256]{1,0:T(8,128)(2,1)S(1)}, bf16[384,256]{1,0:T(8,128)(2,1)S(1)}, u32[]{:S(2)}, u32[]{:S(2)}) collective-permute-start(bf16[384,256]{1,0:T(8,128)(2,1)S(1)} %get-tuple-element.65), channel_id=1, source_target_pairs={{6,0},{7,1},{14,8},{15,9},{22,16},{23,17},{30,24},{31,25}} | collective-permute-start | bytes 589832 | tf_op jit(solution)/shard_map/ppermute | solution.py:479
  37.7 5.7 %collective-permute-done.11.refs_3_ = bf16[384,256]{1,0:T(8,128)(2,1)S(1)} collective-permute-done((bf16[384,256]{1,0:T(8,128)(2,1)S(1)}, bf16[384,256]{1,0:T(8,128)(2,1)S(1)}, u32[]{:S(2)}, u32[]{:S(2)}) %collective-permute-start.11) | collective-permute-done | bytes 196640 | tf_op jit(solution)/shard_map/ppermute | solution.py:479
  43.5 9.7 %collective-permute-done.12.refs_4_ = bf16[384,256]{1,0:T(8,128)(2,1)S(1)} collective-permute-done((bf16[384,256]{1,0:T(8,128)(2,1)S(1)}, bf16[384,256]{1,0:T(8,128)(2,1)S(1)}, u32[]{:S(2)}, u32[]{:S(2)}) %collective-permute-start.12) | collective-permute-done | bytes 196640 | tf_op jit(solution)/shard_map/ppermute | solution.py:479
  53.2 0.0 collective-permute-done.13.refs_5_
  53.2 0.0 collective-permute-done.10.pair.part
  53.2 0.5 shard_map.91
  53.7 0.1 collective-permute-start.14
  53.8 0.2 shard_map.94
  54.0 0.6 collective-permute-start.16
  54.6 0.6 %collective-permute-done.14.theirs = bf16[256,384]{1,0:T(8,128)(2,1)S(1)} collective-permute-done((bf16[256,384]{1,0:T(8,128)(2,1)S(1)}, bf16[256,384]{1,0:T(8,128)(2,1)S(1)}, u32[]{:S(2)}, u32[]{:S(2)}) %collective-permute-start.14) | collective-permute-done | bytes 196640 | tf_op jit(solution)/shard_map/ppermute | solution.py:475
  55.2 0.8 %shard_map.92 = (bf16[256,512]{1,0:T(8,128)(2,1)}, bf16[1,256]{1,0:T(2,128)(2,1)}) custom-call(s32[1]{0:T(128)} %bitcast.10.s, bf16[256,256]{1,0:T(8,128)(2,1)S(1)} %get-tuple-element.71.mine, f32[256,128]{1,0:T(8,128)S(1)} %get-tuple-element.72.gate_mine, bf16[256,384]{1,0:T(8,128)(2,1)S(1)} %collective-permute-done.14.theirs, ...), custom_call_target="tpu_custom_call" | custom-call | bytes 524288 | tf_op jit(solution)/shard_map/pallas_call | solution.py:43
  56.0 0.9 %collective-permute-done.9.part = bf16[384,768]{1,0:T(8,128)(2,1)S(1)} collective-permute-done((bf16[384,768]{1,0:T(8,128)(2,1)S(1)}, bf16[384,768]{1,0:T(8,128)(2,1)S(1)}, u32[]{:S(2)}, u32[]{:S(2)}) %collective-permute-start.9) | collective-permute-done | bytes 589856 | tf_op jit(solution)/shard_map/ppermute | solution.py:482
  57.0 0.2 shard_map.93
  57.2 0.1 collective-permute-start.15
  57.3 0.0 collective-permute-done.16.refs_2_
  57.3 0.9 %shard_map.95.refs_3_ = bf16[256,3072]{1,0:T(8,128)(2,1)} custom-call(s32[1]{0:T(128)} %bitcast.13.refs_0_, bf16[256,768]{1,0:T(8,128)(2,1)S(1)} %get-tuple-element.79.refs_1_, bf16[256,768]{1,0:T(8,128)(2,1)S(1)} %collective-permute-done.16.refs_2_), custom_call_target="tpu_custom_call" | custom-call | bytes 1572864 | tf_op jit(solution)/shard_map/pallas_call | solution.py:43
  58.2 0.8 %collective-permute-done.15.refs_2_ = bf16[256,768]{1,0:T(8,128)(2,1)S(1)} collective-permute-done((bf16[256,768]{1,0:T(8,128)(2,1)S(1)}, bf16[256,768]{1,0:T(8,128)(2,1)S(1)}, u32[]{:S(2)}, u32[]{:S(2)}) %collective-permute-start.15) | collective-permute-done | bytes 393248 | tf_op jit(solution)/shard_map/ppermute | solution.py:475
  59.0 0.9 %shard_map.96 = bf16[256,3072]{1,0:T(8,128)(2,1)} custom-call(s32[1]{0:T(128)} %bitcast.14.refs_0_, bf16[256,768]{1,0:T(8,128)(2,1)S(1)} %get-tuple-element.77.refs_1_, bf16[256,768]{1,0:T(8,128)(2,1)S(1)} %collective-permute-done.15.refs_2_, bf16[256,3072]{1,0:T(8,128)(2,1)} %shard_map.95.refs_3_), custom_call_target="tpu_custom_call", output_to_operand_aliasing={{}: (3, {})} | custom-call | bytes 1572864 | tf_op jit(solution)/shard_map/pallas_call | solution.py:43
  (1 shorter events, 0.0 us)
Async XLA Ops:
  2.4 1.8 %collective-permute-start = (bf16[256,640]{1,0:T(8,128)(2,1)S(1)}, bf16[256,640]{1,0:T(8,128)(2,1)S(1)}, u32[]{:S(2)}, u32[]{:S(2)}) collective-permute-start(bf16[256,640]{1,0:T(8,128)(2,1)S(1)} %get-tuple-element.44), channel_id=1, source_target_pairs={{0,1},{1,0},{2,3},{3,2},{4,5},{5,4},{6,7},{7,6},{8,9},{9,8},{10,11... | collective-permute-start | bytes 983048 | tf_op jit(solution)/shard_map/ppermute | solution.py:475
  4.5 14.1 %collective-permute-start.8 = (bf16[400,256]{1,0:T(8,128)(2,1)S(1)}, bf16[400,256]{1,0:T(8,128)(2,1)S(1)}, u32[]{:S(2)}, u32[]{:S(2)}) collective-permute-start(bf16[400,256]{1,0:T(8,128)(2,1)S(1)} %get-tuple-element.52.refs_7_), channel_id=1, source_target_pairs={{0,6},{1,7},{8,14},{9,15},{16,22},{17,23},{24,30},{25,31}} | collective-permute-start | bytes 614408 | tf_op jit(solution)/shard_map/ppermute | solution.py:479
  10.2 10.3 %collective-permute-start.7 = (bf16[400,256]{1,0:T(8,128)(2,1)S(1)}, bf16[400,256]{1,0:T(8,128)(2,1)S(1)}, u32[]{:S(2)}, u32[]{:S(2)}) collective-permute-start(bf16[400,256]{1,0:T(8,128)(2,1)S(1)} %get-tuple-element.52.refs_7_), channel_id=1, source_target_pairs={{0,4},{1,5},{2,6},{3,7},{8,12},{9,13},{10,14},{11,15},{16,20},{17,... | collective-permute-start | bytes 614408 | tf_op jit(solution)/shard_map/ppermute | solution.py:479
  11.5 11.9 %collective-permute-start.6 = (bf16[400,256]{1,0:T(8,128)(2,1)S(1)}, bf16[400,256]{1,0:T(8,128)(2,1)S(1)}, u32[]{:S(2)}, u32[]{:S(2)}) collective-permute-start(bf16[400,256]{1,0:T(8,128)(2,1)S(1)} %get-tuple-element.52.refs_7_), channel_id=1, source_target_pairs={{0,2},{1,3},{2,4},{3,5},{4,6},{5,7},{8,10},{9,11},{10,12},{11,13},... | collective-permute-start | bytes 614408 | tf_op jit(solution)/shard_map/ppermute | solution.py:479
  14.0 1.2 %collective-permute-start.1 = (bf16[16,128]{1,0:T(8,128)(2,1)S(1)}, bf16[16,128]{1,0:T(8,128)(2,1)S(1)}, u32[]{:S(2)}, u32[]{:S(2)}) collective-permute-start(bf16[16,128]{1,0:T(8,128)(2,1)S(1)} %get-tuple-element.45), channel_id=1, source_target_pairs={{0,1},{1,0},{2,3},{3,2},{4,5},{5,4},{6,7},{7,6},{8,9},{9,8},{10,11... | collective-permute-start | bytes 12296 | tf_op jit(solution)/shard_map/ppermute | solution.py:475
  17.1 6.4 %collective-permute-start.2 = (bf16[256,3072]{1,0:T(8,128)(2,1)S(1)}, bf16[256,3072]{1,0:T(8,128)(2,1)S(1)}, u32[]{:S(2)}, u32[]{:S(2)}) collective-permute-start(bf16[256,3072]{1,0:T(8,128)(2,1)S(1)} %get-tuple-element.49), channel_id=1, source_target_pairs={{0,1},{1,0},{2,3},{3,2},{4,5},{5,4},{6,7},{7,6},{8,9},{9,8},{10,11... | collective-permute-start | bytes 4718600 | tf_op jit(solution)/shard_map/ppermute | solution.py:475
  17.3 10.5 %collective-permute-start.5 = (bf16[400,256]{1,0:T(8,128)(2,1)S(1)}, bf16[400,256]{1,0:T(8,128)(2,1)S(1)}, u32[]{:S(2)}, u32[]{:S(2)}) collective-permute-start(bf16[400,256]{1,0:T(8,128)(2,1)S(1)} %get-tuple-element.51.refs_7_), channel_id=1, source_target_pairs={{0,6},{1,7},{8,14},{9,15},{16,22},{17,23},{24,30},{25,31}} | collective-permute-start | bytes 614408 | tf_op jit(solution)/shard_map/ppermute | solution.py:479
  18.7 9.2 %collective-permute-start.4 = (bf16[400,256]{1,0:T(8,128)(2,1)S(1)}, bf16[400,256]{1,0:T(8,128)(2,1)S(1)}, u32[]{:S(2)}, u32[]{:S(2)}) collective-permute-start(bf16[400,256]{1,0:T(8,128)(2,1)S(1)} %get-tuple-element.51.refs_7_), channel_id=1, source_target_pairs={{0,4},{1,5},{2,6},{3,7},{8,12},{9,13},{10,14},{11,15},{16,20},{17,... | collective-permute-start | bytes 614408 | tf_op jit(solution)/shard_map/ppermute | solution.py:479
  20.5 7.7 %collective-permute-start.3 = (bf16[400,256]{1,0:T(8,128)(2,1)S(1)}, bf16[400,256]{1,0:T(8,128)(2,1)S(1)}, u32[]{:S(2)}, u32[]{:S(2)}) collective-permute-start(bf16[400,256]{1,0:T(8,128)(2,1)S(1)} %get-tuple-element.51.refs_7_), channel_id=1, source_target_pairs={{0,2},{1,3},{2,4},{3,5},{4,6},{5,7},{8,10},{9,11},{10,12},{11,13},... | collective-permute-start | bytes 614408 | tf_op jit(solution)/shard_map/ppermute | solution.py:479
  23.5 4.3 %copy-start = (bf16[256,3072]{1,0:T(8,128)(2,1)}, bf16[256,3072]{1,0:T(8,128)(2,1)S(1)}, u32[]{:S(2)}) copy-start(bf16[256,3072]{1,0:T(8,128)(2,1)S(1)} %collective-permute-done.2.refs_2_.refs_4_) | copy-start | bytes 4718596
  27.8 25.4 %collective-permute-start.10 = (bf16[400,768]{1,0:T(8,128)(2,1)S(1)}, bf16[400,768]{1,0:T(8,128)(2,1)S(1)}, u32[]{:S(2)}, u32[]{:S(2)}) collective-permute-start(bf16[400,768]{1,0:T(8,128)(2,1)S(1)} %get-tuple-element.62), channel_id=1, source_target_pairs={{0,8},{8,16},{16,24},{24,0},{1,9},{9,17},{17,25},{25,1},{2,10},{10... | collective-permute-start | bytes 1843208 | tf_op jit(solution)/shard_map/ppermute | solution.py:482
  33.7 23.2 %collective-permute-start.9 = (bf16[384,768]{1,0:T(8,128)(2,1)S(1)}, bf16[384,768]{1,0:T(8,128)(2,1)S(1)}, u32[]{:S(2)}, u32[]{:S(2)}) collective-permute-start(bf16[384,768]{1,0:T(8,128)(2,1)S(1)} %get-tuple-element.60), channel_id=1, source_target_pairs={{0,8},{8,16},{16,24},{24,0},{1,9},{9,17},{17,25},{25,1},{2,10},{10... | collective-permute-start | bytes 1769480 | tf_op jit(solution)/shard_map/ppermute | solution.py:482
  33.9 9.6 %collective-permute-start.11 = (bf16[384,256]{1,0:T(8,128)(2,1)S(1)}, bf16[384,256]{1,0:T(8,128)(2,1)S(1)}, u32[]{:S(2)}, u32[]{:S(2)}) collective-permute-start(bf16[384,256]{1,0:T(8,128)(2,1)S(1)} %get-tuple-element.63), channel_id=1, source_target_pairs={{2,0},{3,1},{4,2},{5,3},{6,4},{7,5},{10,8},{11,9},{12,10},{13,11},... | collective-permute-start | bytes 589832 | tf_op jit(solution)/shard_map/ppermute | solution.py:479
  35.1 18.0 %collective-permute-start.12 = (bf16[384,256]{1,0:T(8,128)(2,1)S(1)}, bf16[384,256]{1,0:T(8,128)(2,1)S(1)}, u32[]{:S(2)}, u32[]{:S(2)}) collective-permute-start(bf16[384,256]{1,0:T(8,128)(2,1)S(1)} %get-tuple-element.64), channel_id=1, source_target_pairs={{4,0},{5,1},{6,2},{7,3},{12,8},{13,9},{14,10},{15,11},{20,16},{21,... | collective-permute-start | bytes 589832 | tf_op jit(solution)/shard_map/ppermute | solution.py:479
  36.4 16.7 %collective-permute-start.13 = (bf16[384,256]{1,0:T(8,128)(2,1)S(1)}, bf16[384,256]{1,0:T(8,128)(2,1)S(1)}, u32[]{:S(2)}, u32[]{:S(2)}) collective-permute-start(bf16[384,256]{1,0:T(8,128)(2,1)S(1)} %get-tuple-element.65), channel_id=1, source_target_pairs={{6,0},{7,1},{14,8},{15,9},{22,16},{23,17},{30,24},{31,25}} | collective-permute-start | bytes 589832 | tf_op jit(solution)/shard_map/ppermute | solution.py:479
  53.7 1.5 %collective-permute-start.14 = (bf16[256,384]{1,0:T(8,128)(2,1)S(1)}, bf16[256,384]{1,0:T(8,128)(2,1)S(1)}, u32[]{:S(2)}, u32[]{:S(2)}) collective-permute-start(bf16[256,384]{1,0:T(8,128)(2,1)S(1)} %get-tuple-element.73), channel_id=1, source_target_pairs={{0,1},{1,0},{2,3},{3,2},{4,5},{5,4},{6,7},{7,6},{8,9},{9,8},{10,11... | collective-permute-start | bytes 589832 | tf_op jit(solution)/shard_map/ppermute | solution.py:475
  54.0 3.2 %collective-permute-start.16 = (bf16[256,768]{1,0:T(8,128)(2,1)S(1)}, bf16[256,768]{1,0:T(8,128)(2,1)S(1)}, u32[]{:S(2)}, u32[]{:S(2)}) collective-permute-start(bf16[256,768]{1,0:T(8,128)(2,1)S(1)} %get-tuple-element.80), channel_id=1, source_target_pairs={{0,1},{1,0},{2,3},{3,2},{4,5},{5,4},{6,7},{7,6},{8,9},{9,8},{10,11... | collective-permute-start | bytes 1179656 | tf_op jit(solution)/shard_map/ppermute | solution.py:475
  57.2 1.8 %collective-permute-start.15 = (bf16[256,768]{1,0:T(8,128)(2,1)S(1)}, bf16[256,768]{1,0:T(8,128)(2,1)S(1)}, u32[]{:S(2)}, u32[]{:S(2)}) collective-permute-start(bf16[256,768]{1,0:T(8,128)(2,1)S(1)} %get-tuple-element.78), channel_id=1, source_target_pairs={{0,1},{1,0},{2,3},{3,2},{4,5},{5,4},{6,7},{7,6},{8,9},{9,8},{10,11... | collective-permute-start | bytes 1179656 | tf_op jit(solution)/shard_map/ppermute | solution.py:475
where the time goes:
time: 61.2 us; the launch traced here: 60 us
  waiting for transfers between devices  21 us (34%)
  starting transfers between devices  20.7 us (34%)
  Pallas kernels  16.7 us (27%)
  between operations  1.67 us (3%)
    ppermute x9, starting transfers between devices, onward(): lax.ppermute(x, 'ctx', [(i, i + step) for i in range(shards) if 0 <= i +...  18.9 us
    pallas_call x12, Pallas kernels, call(): pl.pallas_call(body, grid_spec=pltpu.PrefetchScalarGridSpec(num_scalar_pr...  16.7 us
    ppermute x9, waiting for transfers between devices, onward(): lax.ppermute(x, 'ctx', [(i, i + step) for i in range(shards) if 0 <= i +...  16.3 us
    ppermute x6, waiting for transfers between devices, swap(): return lax.ppermute(x, 'ctx', [(i, i ^ 1) for i in range(shards)])  3.84 us
    ppermute x6, starting transfers between devices, swap(): return lax.ppermute(x, 'ctx', [(i, i ^ 1) for i in range(shards)])  1.52 us
  transfers between devices with their start and end apart: 17, of which 9 were waited for; matrix products, arithmetic and copies ran while one was open for 0% of the time, Pallas kernels for 24%

commit v1 on v0

--- a/solution.py
+++ b/solution.py
@@ -184,7 +184,7 @@
 def attend_kernel(chips, chunk, has_prior, s, *refs):
     q, qr, cot, cotr, column, columnr = refs[:6]
     at = 6
-    kv = refs[at : at + chips]
+    kv = refs[at : at + 1] + refs[at + 1 : at + chips][::-1]
     at += chips
     prior = refs[at : at + chips] if has_prior else None
     at += chips if has_prior else 0
@@ -478,6 +478,9 @@
         step = by * CORES
         return lax.ppermute(x, "ctx", [(i, i + step) for i in range(shards) if 0 <= i + step < shards])
 
+    def to_later(x):
+        return [onward(x, d) for d in reversed(range(1, chips))][::-1]
+
     def section_on(x):
         return lax.ppermute(x, "section", [(i, (i + 1) % sections) for i in range(sections)])
 
@@ -507,7 +510,7 @@
         tuple(whole((packed_rows, 2 * HEAD_SIZE)) for _ in range(LOCAL_HEADS)) + (whole((META_ROWS, HEAD_SIZE)),),
         moved=4 * packed_rows * HALF_KEY * 2,
     )
-    gathered = [[packed[0]] + [onward(packed[0], d) for d in range(1, chips)]]
+    gathered = [[packed[0]] + to_later(packed[0])]
     own, theirs = call(
         halves_kernel,
         scalars,
@@ -520,14 +523,14 @@
     )
     for h in range(1, LOCAL_HEADS):
         packed[h], theirs = lax.optimization_barrier((packed[h], theirs))
-        gathered.append([packed[h]] + [onward(packed[h], d) for d in range(1, chips)])
+        gathered.append([packed[h]] + to_later(packed[h]))
     swapped = swap(theirs)
     if chips > 1:
-        gathered[0][1:] = passed(scalars, gathered[0][1:])
+        gathered[0][:0:-1] = passed(scalars, gathered[0][:0:-1])
     prior = []
     branches, gate_parts = [], []
     for h in range(LOCAL_HEADS):
-        results = attend(chips, shards, h, scalars, own, swapped, own, swapped, column, other, *gathered[h], *prior)
+        results = attend(chips, shards, h, scalars, own, swapped, own, swapped, column, other, gathered[h][0], *gathered[h][:0:-1], *prior)
         branches.append(section_on(results[0]))
         gate_parts.append(results[1])
         prior = results[2:]

time: 61.2 us -> 62 us (1.013); the launches traced: 60 us -> 61.6 us
  starting transfers between devices: 20.7 us -> 27.1 us
  Pallas kernels: 16.7 us -> 13.6 us
  waiting for transfers between devices: 21 us -> 19.2 us
    ppermute x9, waiting for transfers between devices: 16.3 us -> 10.7 us  [onward(): lax.ppermute(x, 'ctx', [(i, i + step) for i in range(shards) if 0 <= i +...]
    ppermute x2, starting transfers between devices: 0.28 us -> 4.74 us  [section_on(): lax.ppermute(x, 'section', [(i, (i + 1) % sections) for i in range(sectio...]
    ppermute x2, waiting for transfers between devices: 0.92 us -> 4.73 us  [section_on(): lax.ppermute(x, 'section', [(i, (i + 1) % sections) for i in range(sectio...]
    pallas_call x12, Pallas kernels: 16.7 us -> 13.6 us  [call(): pl.pallas_call(body, grid_spec=pltpu.PrefetchScalarGridSpec(num_scalar_pr...]
    ppermute x9, starting transfers between devices: 18.9 us -> 20.9 us  [onward(): lax.ppermute(x, 'ctx', [(i, i + step) for i in range(shards) if 0 <= i +...]
  transfers between devices with their start and end apart: 17 -> 17, of which waited for: 9 -> 7; matrix products, arithmetic and copies ran while one was open for 0% -> 0% of each run, Pallas kernels for 24% -> 18%
where the time goes in v1:
time: 62 us; the launch traced here: 61.6 us
  starting transfers between devices  27.1 us (44%)
  waiting for transfers between devices  19.2 us (31%)
  Pallas kernels  13.6 us (22%)
  between operations  1.68 us (3%)
    ppermute x9, starting transfers between devices, onward(): lax.ppermute(x, 'ctx', [(i, i + step) for i in range(shards) if 0 <= i +...  20.9 us
    pallas_call x12, Pallas kernels, call(): pl.pallas_call(body, grid_spec=pltpu.PrefetchScalarGridSpec(num_scalar_pr...  13.6 us
    ppermute x9, waiting for transfers between devices, onward(): lax.ppermute(x, 'ctx', [(i, i + step) for i in range(shards) if 0 <= i +...  10.7 us
    ppermute x2, starting transfers between devices, section_on(): lax.ppermute(x, 'section', [(i, (i + 1) % sections) for i in range(sectio...  4.74 us
    ppermute x2, waiting for transfers between devices, section_on(): lax.ppermute(x, 'section', [(i, (i + 1) % sections) for i in range(sectio...  4.73 us
    ppermute x6, waiting for transfers between devices, swap(): return lax.ppermute(x, 'ctx', [(i, i ^ 1) for i in range(shards)])  3.84 us
    ppermute x6, starting transfers between devices, swap(): return lax.ppermute(x, 'ctx', [(i, i ^ 1) for i in range(shards)])  1.52 us
  transfers between devices with their start and end apart: 17, of which 7 were waited for; matrix products, arithmetic and copies ran while one was open for 0% of the time, Pallas kernels for 18%

profile of v1, /device:TPU:0, one launch (start us, length us, event | category | flops | bytes accessed | tf_op | source)
XLA Modules:
  0.0 61.6 jit_solution(2832049618415149164)
XLA Ops:
  1.3 1.2 %shard_map.85 = (bf16[256,640]{1,0:T(8,128)(2,1)S(1)}, bf16[256,128]{1,0:T(8,128)(2,1)S(1)}, bf16[256,512]{1,0:T(8,128)(2,1)S(1)}) custom-call(s32[1]{0:T(128)} %bitcast.3.s, bf16[1,256,512]{2,1,0:T(8,128)(2,1)} %k.1, bf16[1,256,512]{2,1,0:T(8,128)(2,1)} %v.1, bf16[1,256]{1,0:T(2,128)(2,1)} %logits.1), custom_call_target="tpu_custom_call" | custom-call | bytes 1310720 | tf_op jit(solution)/shard_map/pallas_call | solution.py:43
  2.4 0.5 collective-permute-start
  3.0 1.3 %collective-permute-done.kr.vr.meta.refs_6_.refs_1_ = bf16[256,640]{1,0:T(8,128)(2,1)S(1)} collective-permute-done((bf16[256,640]{1,0:T(8,128)(2,1)S(1)}, bf16[256,640]{1,0:T(8,128)(2,1)S(1)}, u32[]{:S(2)}, u32[]{:S(2)}) %collective-permute-start) | collective-permute-done | bytes 327712 | tf_op jit(solution)/shard_map/ppermute | solution.py:475
  4.2 0.3 shard_map.86
  4.5 4.8 %collective-permute-start.8 = (bf16[400,256]{1,0:T(8,128)(2,1)S(1)}, bf16[400,256]{1,0:T(8,128)(2,1)S(1)}, u32[]{:S(2)}, u32[]{:S(2)}) collective-permute-start(bf16[400,256]{1,0:T(8,128)(2,1)S(1)} %get-tuple-element.52.refs_7_), channel_id=1, source_target_pairs={{0,2},{1,3},{2,4},{3,5},{4,6},{5,7},{8,10},{9,11},{10,12},{11,13},... | collective-permute-start | bytes 614408 | tf_op jit(solution)/shard_map/ppermute | solution.py:479
  9.3 3.4 %collective-permute-start.7 = (bf16[400,256]{1,0:T(8,128)(2,1)S(1)}, bf16[400,256]{1,0:T(8,128)(2,1)S(1)}, u32[]{:S(2)}, u32[]{:S(2)}) collective-permute-start(bf16[400,256]{1,0:T(8,128)(2,1)S(1)} %get-tuple-element.52.refs_7_), channel_id=1, source_target_pairs={{0,4},{1,5},{2,6},{3,7},{8,12},{9,13},{10,14},{11,15},{16,20},{17,... | collective-permute-start | bytes 614408 | tf_op jit(solution)/shard_map/ppermute | solution.py:479
  12.7 1.3 %collective-permute-start.6 = (bf16[400,256]{1,0:T(8,128)(2,1)S(1)}, bf16[400,256]{1,0:T(8,128)(2,1)S(1)}, u32[]{:S(2)}, u32[]{:S(2)}) collective-permute-start(bf16[400,256]{1,0:T(8,128)(2,1)S(1)} %get-tuple-element.52.refs_7_), channel_id=1, source_target_pairs={{0,6},{1,7},{8,14},{9,15},{16,22},{17,23},{24,30},{25,31}} | collective-permute-start | bytes 614408 | tf_op jit(solution)/shard_map/ppermute | solution.py:479
  14.0 0.1 collective-permute-start.1
  14.1 1.2 %collective-permute-done.1.after = bf16[16,128]{1,0:T(8,128)(2,1)S(1)} collective-permute-done((bf16[16,128]{1,0:T(8,128)(2,1)S(1)}, bf16[16,128]{1,0:T(8,128)(2,1)S(1)}, u32[]{:S(2)}, u32[]{:S(2)}) %collective-permute-start.1) | collective-permute-done | bytes 4128 | tf_op jit(solution)/shard_map/ppermute | solution.py:475
  15.2 1.9 %shard_map.87 = (bf16[256,3072]{1,0:T(8,128)(2,1)S(1)}, bf16[256,3072]{1,0:T(8,128)(2,1)S(1)}) custom-call(s32[1]{0:T(128)} %bitcast.5.s, bf16[1,256,3072]{2,1,0:T(8,128)(2,1)} %q.1, bf16[1,256,3072]{2,1,0:T(8,128)(2,1)} %cot.1, bf16[16,128]{1,0:T(8,128)(2,1)S(1)} %collective-permute-done.1.after), custom_call_target="tpu_custom_call" | custom-call | tf_op jit(solution)/shard_map/pallas_call | solution.py:43
  17.1 0.2 collective-permute-start.2
  17.3 1.3 %collective-permute-start.5 = (bf16[400,256]{1,0:T(8,128)(2,1)S(1)}, bf16[400,256]{1,0:T(8,128)(2,1)S(1)}, u32[]{:S(2)}, u32[]{:S(2)}) collective-permute-start(bf16[400,256]{1,0:T(8,128)(2,1)S(1)} %get-tuple-element.51.refs_7_), channel_id=1, source_target_pairs={{0,2},{1,3},{2,4},{3,5},{4,6},{5,7},{8,10},{9,11},{10,12},{11,13},... | collective-permute-start | bytes 614408 | tf_op jit(solution)/shard_map/ppermute | solution.py:479
  18.6 0.0 collective-permute-done.8.refs_2_
  18.7 1.3 %collective-permute-start.4 = (bf16[400,256]{1,0:T(8,128)(2,1)S(1)}, bf16[400,256]{1,0:T(8,128)(2,1)S(1)}, u32[]{:S(2)}, u32[]{:S(2)}) collective-permute-start(bf16[400,256]{1,0:T(8,128)(2,1)S(1)} %get-tuple-element.51.refs_7_), channel_id=1, source_target_pairs={{0,4},{1,5},{2,6},{3,7},{8,12},{9,13},{10,14},{11,15},{16,20},{17,... | collective-permute-start | bytes 614408 | tf_op jit(solution)/shard_map/ppermute | solution.py:479
  20.0 0.0 collective-permute-done.7.refs_1_
  20.0 4.9 %collective-permute-start.3 = (bf16[400,256]{1,0:T(8,128)(2,1)S(1)}, bf16[400,256]{1,0:T(8,128)(2,1)S(1)}, u32[]{:S(2)}, u32[]{:S(2)}) collective-permute-start(bf16[400,256]{1,0:T(8,128)(2,1)S(1)} %get-tuple-element.51.refs_7_), channel_id=1, source_target_pairs={{0,6},{1,7},{8,14},{9,15},{16,22},{17,23},{24,30},{25,31}} | collective-permute-start | bytes 614408 | tf_op jit(solution)/shard_map/ppermute | solution.py:479
  24.9 0.0 collective-permute-done.6.refs_0_
  24.9 0.0 collective-permute-done.2.refs_2_.refs_4_
  24.9 0.0 copy-start
  24.9 2.8 %shard_map.89 = (bf16[400,768]{1,0:T(8,128)(2,1)S(1)}, f32[384,128]{1,0:T(8,128)S(1)}, f32[384,128]{1,0:T(8,128)S(1)}, bf16[384,128]{1,0:T(8,128)(2,1)S(1)}, bf1...) custom-call(s32[1]{0:T(128)} %bitcast.7.refs_0_, bf16[256,3072]{1,0:T(8,128)(2,1)S(1)} %get-tuple-element.46.refs_1_.refs_3_, ...), custom_call_target="tpu_custom_call" | custom-call | flops 10066329600 | bytes 1843200 | tf_op jit(solution)/shard_map/pallas_call | solution.py:43
  27.7 0.0 copy-done
  27.7 3.1 %collective-permute-start.10 = (bf16[400,768]{1,0:T(8,128)(2,1)S(1)}, bf16[400,768]{1,0:T(8,128)(2,1)S(1)}, u32[]{:S(2)}, u32[]{:S(2)}) collective-permute-start(bf16[400,768]{1,0:T(8,128)(2,1)S(1)} %get-tuple-element.62), channel_id=1, source_target_pairs={{0,8},{8,16},{16,24},{24,0},{1,9},{9,17},{17,25},{25,1},{2,10},{10... | collective-permute-start | bytes 1843208 | tf_op jit(solution)/shard_map/ppermute | solution.py:485
  30.8 0.0 collective-permute-done.5.refs_10_
  30.8 0.0 collective-permute-done.4.refs_9_
  30.8 0.0 collective-permute-done.3.refs_8_
  30.9 4.1 %shard_map.90 = (bf16[384,768]{1,0:T(8,128)(2,1)S(1)}, f32[384,128]{1,0:T(8,128)S(1)}, f32[384,256]{1,0:T(8,128)S(1)}, bf16[384,256]{1,0:T(8,128)(2,1)S(1)}, bf1...) custom-call(s32[1]{0:T(128)} %bitcast.8.refs_0_, bf16[256,3072]{1,0:T(8,128)(2,1)S(1)} %get-tuple-element.46.refs_1_.refs_3_, ...), custom_call_target="tpu_custom_call" | custom-call | flops 10066329600 | bytes 1843200 | tf_op jit(solution)/shard_map/pallas_call | solution.py:43
  34.9 1.6 %collective-permute-start.9 = (bf16[384,768]{1,0:T(8,128)(2,1)S(1)}, bf16[384,768]{1,0:T(8,128)(2,1)S(1)}, u32[]{:S(2)}, u32[]{:S(2)}) collective-permute-start(bf16[384,768]{1,0:T(8,128)(2,1)S(1)} %get-tuple-element.60), channel_id=1, source_target_pairs={{0,8},{8,16},{16,24},{24,0},{1,9},{9,17},{17,25},{25,1},{2,10},{10... | collective-permute-start | bytes 1769480 | tf_op jit(solution)/shard_map/ppermute | solution.py:485
  36.5 1.3 %collective-permute-start.11 = (bf16[384,256]{1,0:T(8,128)(2,1)S(1)}, bf16[384,256]{1,0:T(8,128)(2,1)S(1)}, u32[]{:S(2)}, u32[]{:S(2)}) collective-permute-start(bf16[384,256]{1,0:T(8,128)(2,1)S(1)} %get-tuple-element.63), channel_id=1, source_target_pairs={{2,0},{3,1},{4,2},{5,3},{6,4},{7,5},{10,8},{11,9},{12,10},{13,11},... | collective-permute-start | bytes 589832 | tf_op jit(solution)/shard_map/ppermute | solution.py:479
  37.8 1.3 %collective-permute-start.12 = (bf16[384,256]{1,0:T(8,128)(2,1)S(1)}, bf16[384,256]{1,0:T(8,128)(2,1)S(1)}, u32[]{:S(2)}, u32[]{:S(2)}) collective-permute-start(bf16[384,256]{1,0:T(8,128)(2,1)S(1)} %get-tuple-element.64), channel_id=1, source_target_pairs={{4,0},{5,1},{6,2},{7,3},{12,8},{13,9},{14,10},{15,11},{20,16},{21,... | collective-permute-start | bytes 589832 | tf_op jit(solution)/shard_map/ppermute | solution.py:479
  39.1 1.3 %collective-permute-start.13 = (bf16[384,256]{1,0:T(8,128)(2,1)S(1)}, bf16[384,256]{1,0:T(8,128)(2,1)S(1)}, u32[]{:S(2)}, u32[]{:S(2)}) collective-permute-start(bf16[384,256]{1,0:T(8,128)(2,1)S(1)} %get-tuple-element.65), channel_id=1, source_target_pairs={{6,0},{7,1},{14,8},{15,9},{22,16},{23,17},{30,24},{31,25}} | collective-permute-start | bytes 589832 | tf_op jit(solution)/shard_map/ppermute | solution.py:479
  40.4 3.7 %collective-permute-done.11.refs_3_ = bf16[384,256]{1,0:T(8,128)(2,1)S(1)} collective-permute-done((bf16[384,256]{1,0:T(8,128)(2,1)S(1)}, bf16[384,256]{1,0:T(8,128)(2,1)S(1)}, u32[]{:S(2)}, u32[]{:S(2)}) %collective-permute-start.11) | collective-permute-done | bytes 196640 | tf_op jit(solution)/shard_map/ppermute | solution.py:479
  44.1 7.0 %collective-permute-done.12.refs_4_ = bf16[384,256]{1,0:T(8,128)(2,1)S(1)} collective-permute-done((bf16[384,256]{1,0:T(8,128)(2,1)S(1)}, bf16[384,256]{1,0:T(8,128)(2,1)S(1)}, u32[]{:S(2)}, u32[]{:S(2)}) %collective-permute-start.12) | collective-permute-done | bytes 196640 | tf_op jit(solution)/shard_map/ppermute | solution.py:479
  51.1 0.0 collective-permute-done.13.refs_5_
  51.1 0.0 collective-permute-done.10.pair.part
  51.1 0.4 shard_map.91
  51.5 0.1 collective-permute-start.14
  51.6 0.2 shard_map.94
  51.8 0.6 collective-permute-start.16
  52.4 0.6 %collective-permute-done.14.theirs = bf16[256,384]{1,0:T(8,128)(2,1)S(1)} collective-permute-done((bf16[256,384]{1,0:T(8,128)(2,1)S(1)}, bf16[256,384]{1,0:T(8,128)(2,1)S(1)}, u32[]{:S(2)}, u32[]{:S(2)}) %collective-permute-start.14) | collective-permute-done | bytes 196640 | tf_op jit(solution)/shard_map/ppermute | solution.py:475
  53.0 0.8 %shard_map.92 = (bf16[256,512]{1,0:T(8,128)(2,1)}, bf16[1,256]{1,0:T(2,128)(2,1)}) custom-call(s32[1]{0:T(128)} %bitcast.10.s, bf16[256,256]{1,0:T(8,128)(2,1)S(1)} %get-tuple-element.71.mine, f32[256,128]{1,0:T(8,128)S(1)} %get-tuple-element.72.gate_mine, bf16[256,384]{1,0:T(8,128)(2,1)S(1)} %collective-permute-done.14.theirs, ...), custom_call_target="tpu_custom_call" | custom-call | bytes 524288 | tf_op jit(solution)/shard_map/pallas_call | solution.py:43
  53.8 4.7 %collective-permute-done.9.part = bf16[384,768]{1,0:T(8,128)(2,1)S(1)} collective-permute-done((bf16[384,768]{1,0:T(8,128)(2,1)S(1)}, bf16[384,768]{1,0:T(8,128)(2,1)S(1)}, u32[]{:S(2)}, u32[]{:S(2)}) %collective-permute-start.9) | collective-permute-done | bytes 589856 | tf_op jit(solution)/shard_map/ppermute | solution.py:485
  58.6 0.2 shard_map.93
  58.8 0.1 collective-permute-start.15
  58.9 0.0 collective-permute-done.16.refs_2_
  58.9 0.9 %shard_map.95.refs_3_ = bf16[256,3072]{1,0:T(8,128)(2,1)} custom-call(s32[1]{0:T(128)} %bitcast.13.refs_0_, bf16[256,768]{1,0:T(8,128)(2,1)S(1)} %get-tuple-element.79.refs_1_, bf16[256,768]{1,0:T(8,128)(2,1)S(1)} %collective-permute-done.16.refs_2_), custom_call_target="tpu_custom_call" | custom-call | bytes 1572864 | tf_op jit(solution)/shard_map/pallas_call | solution.py:43
  59.8 0.8 %collective-permute-done.15.refs_2_ = bf16[256,768]{1,0:T(8,128)(2,1)S(1)} collective-permute-done((bf16[256,768]{1,0:T(8,128)(2,1)S(1)}, bf16[256,768]{1,0:T(8,128)(2,1)S(1)}, u32[]{:S(2)}, u32[]{:S(2)}) %collective-permute-start.15) | collective-permute-done | bytes 393248 | tf_op jit(solution)/shard_map/ppermute | solution.py:475
  60.6 0.9 %shard_map.96 = bf16[256,3072]{1,0:T(8,128)(2,1)} custom-call(s32[1]{0:T(128)} %bitcast.14.refs_0_, bf16[256,768]{1,0:T(8,128)(2,1)S(1)} %get-tuple-element.77.refs_1_, bf16[256,768]{1,0:T(8,128)(2,1)S(1)} %collective-permute-done.15.refs_2_, bf16[256,3072]{1,0:T(8,128)(2,1)} %shard_map.95.refs_3_), custom_call_target="tpu_custom_call", output_to_operand_aliasing={{}: (3, {})} | custom-call | bytes 1572864 | tf_op jit(solution)/shard_map/pallas_call | solution.py:43
  (1 shorter events, 0.0 us)
Async XLA Ops:
  2.4 1.8 %collective-permute-start = (bf16[256,640]{1,0:T(8,128)(2,1)S(1)}, bf16[256,640]{1,0:T(8,128)(2,1)S(1)}, u32[]{:S(2)}, u32[]{:S(2)}) collective-permute-start(bf16[256,640]{1,0:T(8,128)(2,1)S(1)} %get-tuple-element.44), channel_id=1, source_target_pairs={{0,1},{1,0},{2,3},{3,2},{4,5},{5,4},{6,7},{7,6},{8,9},{9,8},{10,11... | collective-permute-start | bytes 983048 | tf_op jit(solution)/shard_map/ppermute | solution.py:475
  4.5 14.2 %collective-permute-start.8 = (bf16[400,256]{1,0:T(8,128)(2,1)S(1)}, bf16[400,256]{1,0:T(8,128)(2,1)S(1)}, u32[]{:S(2)}, u32[]{:S(2)}) collective-permute-start(bf16[400,256]{1,0:T(8,128)(2,1)S(1)} %get-tuple-element.52.refs_7_), channel_id=1, source_target_pairs={{0,2},{1,3},{2,4},{3,5},{4,6},{5,7},{8,10},{9,11},{10,12},{11,13},... | collective-permute-start | bytes 614408 | tf_op jit(solution)/shard_map/ppermute | solution.py:479
  9.3 10.7 %collective-permute-start.7 = (bf16[400,256]{1,0:T(8,128)(2,1)S(1)}, bf16[400,256]{1,0:T(8,128)(2,1)S(1)}, u32[]{:S(2)}, u32[]{:S(2)}) collective-permute-start(bf16[400,256]{1,0:T(8,128)(2,1)S(1)} %get-tuple-element.52.refs_7_), channel_id=1, source_target_pairs={{0,4},{1,5},{2,6},{3,7},{8,12},{9,13},{10,14},{11,15},{16,20},{17,... | collective-permute-start | bytes 614408 | tf_op jit(solution)/shard_map/ppermute | solution.py:479
  12.7 12.2 %collective-permute-start.6 = (bf16[400,256]{1,0:T(8,128)(2,1)S(1)}, bf16[400,256]{1,0:T(8,128)(2,1)S(1)}, u32[]{:S(2)}, u32[]{:S(2)}) collective-permute-start(bf16[400,256]{1,0:T(8,128)(2,1)S(1)} %get-tuple-element.52.refs_7_), channel_id=1, source_target_pairs={{0,6},{1,7},{8,14},{9,15},{16,22},{17,23},{24,30},{25,31}} | collective-permute-start | bytes 614408 | tf_op jit(solution)/shard_map/ppermute | solution.py:479
  14.0 1.2 %collective-permute-start.1 = (bf16[16,128]{1,0:T(8,128)(2,1)S(1)}, bf16[16,128]{1,0:T(8,128)(2,1)S(1)}, u32[]{:S(2)}, u32[]{:S(2)}) collective-permute-start(bf16[16,128]{1,0:T(8,128)(2,1)S(1)} %get-tuple-element.45), channel_id=1, source_target_pairs={{0,1},{1,0},{2,3},{3,2},{4,5},{5,4},{6,7},{7,6},{8,9},{9,8},{10,11... | collective-permute-start | bytes 12296 | tf_op jit(solution)/shard_map/ppermute | solution.py:475
  17.1 7.8 %collective-permute-start.2 = (bf16[256,3072]{1,0:T(8,128)(2,1)S(1)}, bf16[256,3072]{1,0:T(8,128)(2,1)S(1)}, u32[]{:S(2)}, u32[]{:S(2)}) collective-permute-start(bf16[256,3072]{1,0:T(8,128)(2,1)S(1)} %get-tuple-element.49), channel_id=1, source_target_pairs={{0,1},{1,0},{2,3},{3,2},{4,5},{5,4},{6,7},{7,6},{8,9},{9,8},{10,11... | collective-permute-start | bytes 4718600 | tf_op jit(solution)/shard_map/ppermute | solution.py:475
  17.3 13.5 %collective-permute-start.5 = (bf16[400,256]{1,0:T(8,128)(2,1)S(1)}, bf16[400,256]{1,0:T(8,128)(2,1)S(1)}, u32[]{:S(2)}, u32[]{:S(2)}) collective-permute-start(bf16[400,256]{1,0:T(8,128)(2,1)S(1)} %get-tuple-element.51.refs_7_), channel_id=1, source_target_pairs={{0,2},{1,3},{2,4},{3,5},{4,6},{5,7},{8,10},{9,11},{10,12},{11,13},... | collective-permute-start | bytes 614408 | tf_op jit(solution)/shard_map/ppermute | solution.py:479
  18.7 12.2 %collective-permute-start.4 = (bf16[400,256]{1,0:T(8,128)(2,1)S(1)}, bf16[400,256]{1,0:T(8,128)(2,1)S(1)}, u32[]{:S(2)}, u32[]{:S(2)}) collective-permute-start(bf16[400,256]{1,0:T(8,128)(2,1)S(1)} %get-tuple-element.51.refs_7_), channel_id=1, source_target_pairs={{0,4},{1,5},{2,6},{3,7},{8,12},{9,13},{10,14},{11,15},{16,20},{17,... | collective-permute-start | bytes 614408 | tf_op jit(solution)/shard_map/ppermute | solution.py:479
  20.0 10.9 %collective-permute-start.3 = (bf16[400,256]{1,0:T(8,128)(2,1)S(1)}, bf16[400,256]{1,0:T(8,128)(2,1)S(1)}, u32[]{:S(2)}, u32[]{:S(2)}) collective-permute-start(bf16[400,256]{1,0:T(8,128)(2,1)S(1)} %get-tuple-element.51.refs_7_), channel_id=1, source_target_pairs={{0,6},{1,7},{8,14},{9,15},{16,22},{17,23},{24,30},{25,31}} | collective-permute-start | bytes 614408 | tf_op jit(solution)/shard_map/ppermute | solution.py:479
  24.9 2.8 %copy-start = (bf16[256,3072]{1,0:T(8,128)(2,1)}, bf16[256,3072]{1,0:T(8,128)(2,1)S(1)}, u32[]{:S(2)}) copy-start(bf16[256,3072]{1,0:T(8,128)(2,1)S(1)} %collective-permute-done.2.refs_2_.refs_4_) | copy-start | bytes 4718596
  27.7 23.4 %collective-permute-start.10 = (bf16[400,768]{1,0:T(8,128)(2,1)S(1)}, bf16[400,768]{1,0:T(8,128)(2,1)S(1)}, u32[]{:S(2)}, u32[]{:S(2)}) collective-permute-start(bf16[400,768]{1,0:T(8,128)(2,1)S(1)} %get-tuple-element.62), channel_id=1, source_target_pairs={{0,8},{8,16},{16,24},{24,0},{1,9},{9,17},{17,25},{25,1},{2,10},{10... | collective-permute-start | bytes 1843208 | tf_op jit(solution)/shard_map/ppermute | solution.py:485
  34.9 23.6 %collective-permute-start.9 = (bf16[384,768]{1,0:T(8,128)(2,1)S(1)}, bf16[384,768]{1,0:T(8,128)(2,1)S(1)}, u32[]{:S(2)}, u32[]{:S(2)}) collective-permute-start(bf16[384,768]{1,0:T(8,128)(2,1)S(1)} %get-tuple-element.60), channel_id=1, source_target_pairs={{0,8},{8,16},{16,24},{24,0},{1,9},{9,17},{17,25},{25,1},{2,10},{10... | collective-permute-start | bytes 1769480 | tf_op jit(solution)/shard_map/ppermute | solution.py:485
  36.5 7.6 %collective-permute-start.11 = (bf16[384,256]{1,0:T(8,128)(2,1)S(1)}, bf16[384,256]{1,0:T(8,128)(2,1)S(1)}, u32[]{:S(2)}, u32[]{:S(2)}) collective-permute-start(bf16[384,256]{1,0:T(8,128)(2,1)S(1)} %get-tuple-element.63), channel_id=1, source_target_pairs={{2,0},{3,1},{4,2},{5,3},{6,4},{7,5},{10,8},{11,9},{12,10},{13,11},... | collective-permute-start | bytes 589832 | tf_op jit(solution)/shard_map/ppermute | solution.py:479
  37.8 13.2 %collective-permute-start.12 = (bf16[384,256]{1,0:T(8,128)(2,1)S(1)}, bf16[384,256]{1,0:T(8,128)(2,1)S(1)}, u32[]{:S(2)}, u32[]{:S(2)}) collective-permute-start(bf16[384,256]{1,0:T(8,128)(2,1)S(1)} %get-tuple-element.64), channel_id=1, source_target_pairs={{4,0},{5,1},{6,2},{7,3},{12,8},{13,9},{14,10},{15,11},{20,16},{21,... | collective-permute-start | bytes 589832 | tf_op jit(solution)/shard_map/ppermute | solution.py:479
  39.1 11.9 %collective-permute-start.13 = (bf16[384,256]{1,0:T(8,128)(2,1)S(1)}, bf16[384,256]{1,0:T(8,128)(2,1)S(1)}, u32[]{:S(2)}, u32[]{:S(2)}) collective-permute-start(bf16[384,256]{1,0:T(8,128)(2,1)S(1)} %get-tuple-element.65), channel_id=1, source_target_pairs={{6,0},{7,1},{14,8},{15,9},{22,16},{23,17},{30,24},{31,25}} | collective-permute-start | bytes 589832 | tf_op jit(solution)/shard_map/ppermute | solution.py:479
  51.5 1.5 %collective-permute-start.14 = (bf16[256,384]{1,0:T(8,128)(2,1)S(1)}, bf16[256,384]{1,0:T(8,128)(2,1)S(1)}, u32[]{:S(2)}, u32[]{:S(2)}) collective-permute-start(bf16[256,384]{1,0:T(8,128)(2,1)S(1)} %get-tuple-element.73), channel_id=1, source_target_pairs={{0,1},{1,0},{2,3},{3,2},{4,5},{5,4},{6,7},{7,6},{8,9},{9,8},{10,11... | collective-permute-start | bytes 589832 | tf_op jit(solution)/shard_map/ppermute | solution.py:475
  51.8 7.1 %collective-permute-start.16 = (bf16[256,768]{1,0:T(8,128)(2,1)S(1)}, bf16[256,768]{1,0:T(8,128)(2,1)S(1)}, u32[]{:S(2)}, u32[]{:S(2)}) collective-permute-start(bf16[256,768]{1,0:T(8,128)(2,1)S(1)} %get-tuple-element.80), channel_id=1, source_target_pairs={{0,1},{1,0},{2,3},{3,2},{4,5},{5,4},{6,7},{7,6},{8,9},{9,8},{10,11... | collective-permute-start | bytes 1179656 | tf_op jit(solution)/shard_map/ppermute | solution.py:475
  58.8 1.8 %collective-permute-start.15 = (bf16[256,768]{1,0:T(8,128)(2,1)S(1)}, bf16[256,768]{1,0:T(8,128)(2,1)S(1)}, u32[]{:S(2)}, u32[]{:S(2)}) collective-permute-start(bf16[256,768]{1,0:T(8,128)(2,1)S(1)} %get-tuple-element.78), channel_id=1, source_target_pairs={{0,1},{1,0},{2,3},{3,2},{4,5},{5,4},{6,7},{7,6},{8,9},{9,8},{10,11... | collective-permute-start | bytes 1179656 | tf_op jit(solution)/shard_map/ppermute | solution.py:475
